TPU v7x, 768 devices: a whole 4x8x12 slice. The times are simulated.
768 devices in a mesh: dp: 8 (over y_hi, core), basis: 96 (over x, y_lo, z).
Axes of the slice: x: 4, y: 8 (y_hi: 4, y_lo: 2; y = y_hi * 2 + y_lo), z: 12, core: 2. Of those that a mesh axis runs over, the one named last changes fastest.
Arguments:
- out_grads: bfloat16 [15360, 2048], P(('dp', 'basis')), may hold values from -6 to 6
- inputs: bfloat16 [2048, 6144], P('dp'), may hold values from -6 to 6
- basis_grads: bfloat16 [15360, 15360], P('dp', 'basis'), may hold values from -0.046875 to 0.046875
- basis_inputs: bfloat16 [6144, 6144], P(None, 'basis'), may hold values from -0.078125 to 0.078125
- counts: int32 [16], P('dp'), may hold values from 1 to 128, 1536 in all
Outputs:
- corrections: float32 [15360, 6144], P('basis', 'dp')
Inputs may be any that keep to these rules, and one draw needn't show every extreme that they name: `counts`: some example has all 128 slots live.
All inputs are finite; a program needn't handle non-finite values. No bound on the sum of `counts` on one device may be relied on, other than what follows from the above.
Results may differ from a plain program's by a relative error of at most 0.0023.
Values may be sent and summed in bfloat16 or wider, within the bound.
A program may use at most 64 MiB of HBM per device.

v0:
```python
import jax
import jax.numpy as jnp
from jax import lax
from jax.sharding import PartitionSpec as P


def shards(out_grads, inputs, basis_grads, basis_inputs, counts):
    examples_here = counts.shape[0]
    slot_count = inputs.shape[0] // examples_here
    feature_count = inputs.shape[1]
    column_count = basis_grads.shape[1]
    all_examples = examples_here * lax.axis_size("dp")
    factor = 1.0 / (all_examples * slot_count)
    partial_value = lax.dot_general(
        basis_grads,
        lax.all_gather(out_grads, "basis", axis=0, tiled=True),
        (((0,), (0,)), ((), ())),
        preferred_element_type=jnp.float32,
    )
    slots = jnp.arange(slot_count, dtype=jnp.int32)
    keep = slots[None, :] < counts[:, None]
    shaped = inputs.reshape(examples_here, slot_count, feature_count)
    masked = jnp.where(keep[:, :, None], shaped, jnp.zeros((), inputs.dtype)).reshape(
        -1, feature_count
    )
    rotated_inputs = lax.dot_general(
        basis_inputs, masked, (((0,), (1,)), ((), ())), preferred_element_type=jnp.float32
    ).astype(jnp.bfloat16)
    wide_inputs = None
    local_grads = lax.psum_scatter(partial_value, "dp", scatter_dimension=1, tiled=True).astype(
        jnp.bfloat16
    )
    wide_inputs = lax.all_gather(rotated_inputs, "basis", axis=0, tiled=True)
    grad_blocks = local_grads.reshape(column_count, examples_here, slot_count)
    input_blocks = wide_inputs.reshape(feature_count, examples_here, slot_count)
    product = jnp.einsum(
        "jet,ket->ejk", grad_blocks, input_blocks, preferred_element_type=jnp.float32
    )
    squares = jnp.sum(product * product, axis=0)
    total = lax.psum_scatter(squares, "dp", scatter_dimension=1, tiled=True)
    return total * factor


def solution(mesh):
    placed = (P(("dp", "basis"), None), P("dp", None), P("dp", "basis"), P(None, "basis"), P("dp"))
    return jax.shard_map(
        shards, mesh=mesh, in_specs=placed, out_specs=P("basis", "dp"), check_vma=False
    )
```

profile of v0, /device:TPU:1, one launch (start us, length us, event | category | flops | bytes accessed | tf_op | source)
XLA Modules:
  0.0 1044.1 jit_solution(311025836367847974)
XLA Ops:
  6.5 0.0 copy-start
  6.5 0.0 all-gather.6.cloned.1.call-start
  6.5 0.7 all-gather.6.cloned.1.call-update
  7.3 0.0 all-gather.4.cloned.1.call-start
  7.3 0.7 compare_bitcast_fusion
  8.0 0.0 copy-done
  8.0 3.6 fusion.12
  11.7 0.0 all-gather.4.cloned.1.call-update
  11.7 0.0 copy-start.1
  11.7 0.0 reduce-scatter.3.cloned.1.call-start
  11.8 411.0 %all-gather.6.cloned.1.call-done = bf16[96,20,2048]{2,1,0:T(8,128)(2,1)} async-done(((bf16[1,20,2048]{2,1,0:T(8,128)(2,1)}), bf16[96,20,2048]{2,1,0:T(8,128)(2,1)}) %all-gather.6.cloned.1.call-update) | async-done | bytes 7864336 | tf_op jit(solution)/shard_map/all_gather | solution.py:16
  422.8 12.5 %reshape.32 = bf16[1920,2048]{1,0:T(8,128)(2,1)} reshape(bf16[96,20,2048]{2,1,0:T(8,128)(2,1)} %all-gather.6.cloned.1.call-done) | data formatting | bytes 15728640
  435.3 0.0 copy-done.1
  435.3 5.8 fusion.18
  441.1 0.0 reduce-scatter.3.cloned.1.call-update
  441.2 0.0 reduce-scatter.5.cloned.1.call-start
  441.2 424.6 %all-gather.4.cloned.1.call-done = bf16[6144,256]{1,0:T(8,128)(2,1)} async-done(((bf16[64,256]{1,0:T(8,128)(2,1)}), bf16[6144,256]{1,0:T(8,128)(2,1)}) %all-gather.4.cloned.1.call-update) | async-done | bytes 3145744 | tf_op jit(solution)/shard_map/all_gather | solution.py:33
  865.8 103.1 %reduce-scatter.3.cloned.1.call-done = f32[160,256]{1,0:T(8,128)} async-done(((f32[160,2048]{1,0:T(8,128)}), f32[160,256]{1,0:T(8,128)}) %reduce-scatter.3.cloned.1.call-update) | async-done | bytes 163856 | tf_op jit(solution)/shard_map/reduce_scatter | solution.py:30
  968.9 5.4 fusion.5
  974.3 0.0 reduce-scatter.5.cloned.1.call-update
  974.3 61.4 %reduce-scatter.5.cloned.1.call-done = f32[160,768]{1,0:T(8,128)} async-done(((f32[160,6144]{1,0:T(8,128)}), f32[160,768]{1,0:T(8,128)}) %reduce-scatter.5.cloned.1.call-update) | async-done | bytes 491536 | tf_op jit(solution)/shard_map/reduce_scatter | solution.py:40
  1035.7 1.8 broadcast_multiply_fusion
Async XLA Ops:
  6.5 1.5 copy-start
  6.5 416.3 %all-gather.6.cloned.1.call-start = ((), (), s32[]{:S(2)}) async-start(), calls=%async_computation.5 | async-start | bytes 9535488 | tf_op jit(solution)/shard_map/all_gather | solution.py:16
  7.3 858.5 %all-gather.4.cloned.1.call-start = ((), (), s32[]{:S(2)}) async-start(), calls=%async_computation.3 | async-start | bytes 3178496 | tf_op jit(solution)/shard_map/all_gather | solution.py:33
  11.7 423.6 %copy-start.1 = (bf16[1920,160]{0,1:T(8,128)(2,1)S(1)}, bf16[1920,160]{0,1:T(8,128)(2,1)}, u32[]{:S(2)}) copy-start(bf16[1920,160]{0,1:T(8,128)(2,1)} %param.7) | copy-start | bytes 1843204
  11.7 957.2 %reduce-scatter.3.cloned.1.call-start = ((), (), s32[]{:S(2)}) async-start(), calls=%async_computation.2 | async-start | bytes 1474560 | tf_op jit(solution)/shard_map/reduce_scatter | solution.py:30
  441.2 594.5 %reduce-scatter.5.cloned.1.call-start = ((), (), s32[]{:S(2)}) async-start(), calls=%async_computation.4 | async-start | bytes 4423680 | tf_op jit(solution)/shard_map/reduce_scatter | solution.py:40
Sparse Core Ops, SparseCore 0:
  9.7 413.0 all-gather.5
  425.2 440.5 all-gather.3
  868.9 99.9 reduce-scatter.2
  974.5 61.2 reduce-scatter.4
where the time goes:
time: 1050 us; the launch traced here: 1040 us
  waiting for transfers between devices  1000 us (95%)
  matrix products  14.9 us (1%)
  between operations  13.1 us (1%)
  local copies, waits for them, and re-layouts  12.5 us (1%)
    all_gather x1, waiting for transfers between devices, shards(): wide_inputs = lax.all_gather(rotated_inputs, 'basis', axis=0, tiled=True)  425 us
    all_gather x1, waiting for transfers between devices, shards(): lax.all_gather(out_grads, 'basis', axis=0, tiled=True)  411 us
    reduce_scatter x1, waiting for transfers between devices, shards(): lax.psum_scatter(partial_value, 'dp', scatter_dimension=1, tiled=True)  103 us
    reduce_scatter x1, waiting for transfers between devices, shards(): total = lax.psum_scatter(squares, 'dp', scatter_dimension=1, tiled=True)  61.4 us
  transfers between devices with their start and end apart: 4, of which 4 were waited for; matrix products, arithmetic and copies ran while one was open for 2% of the time, Pallas kernels for 0%

commit v1 on v0

v1 whole, which is shorter than its diff:
```python
import jax
import jax.numpy as jnp
from jax import lax
from jax.experimental import pallas as pl
from jax.experimental.pallas import tpu as pltpu
from jax.sharding import PartitionSpec as P

MESH = pl.DeviceIdType.MESH
BF16, F32 = jnp.bfloat16, jnp.float32

NX, NL, NZ, NH, NC = 4, 2, 12, 4, 2
SLOTS = NL * NZ
UNITS = 20
GROUP = NX * UNITS
BLOCK = SLOTS * GROUP
COLS = 160
HALF = COLS // 2
QUARTER = 512
CHUNKS = 2
TW = QUARTER // CHUNKS
SLOT = 128
FEATS = 64
WIDE = NZ * FEATS
TOK = 256
DEPTH = 6144
FACTOR = 1.0 / 2048.0
NSEM = 128


def dot(a, b, dims=((1,), (0,))):
    return lax.dot_general(a, b, (dims, ((), ())), preferred_element_type=F32)


def kernel(
    g_ref, b_ref, in_ref, bi_ref, cnt_ref, out_ref,
    gs, ga, gb, bb, iv, biv, rt, rb, cb, cr, ss, sr, ab, acc, o1s, o1r, o2s, o2r,
    ssem, rsem, lsem,
):
    d, b = lax.axis_index("dp"), lax.axis_index("basis")
    yh, c = d // NC, d % NC
    x, yl, z = b // SLOTS, (b // NZ) % NL, b % NZ
    slot = yl * NZ + z

    def dev(yh=yh, c=c, x=x, yl=yl, z=z):
        return (yh * NC + c, x * SLOTS + yl * NZ + z)

    zr, zl = lax.rem(z + 1, NZ), lax.rem(z + NZ - 1, NZ)
    xr, xl, xo = lax.rem(x + 1, NX), lax.rem(x + 3, NX), lax.rem(x + 2, NX)
    yhs = [lax.rem(yh + r, NH) for r in range(NH)]
    pair_y, pair_c = dev(yl=1 - yl), dev(c=1 - c)
    right, left = dev(z=zr), dev(z=zl)
    swap = dev(yh=x, c=yl, x=yh, yl=c)
    lone = jnp.logical_and(yh == x, c == yl)

    barrier = pltpu.get_barrier_semaphore()
    peers = [right, left, pair_y, pair_c]
    peers += [dev(x=xr), dev(x=xl), dev(x=xo)] + [dev(yh=yhs[r]) for r in (1, 2, 3)]
    for peer in peers:
        pl.semaphore_signal(barrier, inc=1, device_id=peer, device_id_type=MESH)

    @pl.when(jnp.logical_not(lone))
    def _():
        pl.semaphore_signal(barrier, inc=1, device_id=swap, device_id_type=MESH)

    keys = {}
    sent = []

    def copy(key, src, dst, target):
        i = keys.setdefault(key, len(keys))
        return pltpu.make_async_remote_copy(
            src_ref=src, dst_ref=dst, send_sem=ssem.at[i], recv_sem=rsem.at[i],
            device_id=target, device_id_type=MESH,
        )

    def send(key, src, dst, target):
        cp = copy(key, src, dst, target)
        cp.start()
        sent.append(cp)

    def got(key, ref):
        copy(key, ref, ref, pair_c).wait_recv()

    load_in = pltpu.make_async_copy(in_ref, iv, lsem.at[0])
    load_bi = pltpu.make_async_copy(bi_ref, biv, lsem.at[1])
    load_in.start()
    load_bi.start()

    gs[...] = jnp.zeros_like(gs)
    for q in range(NX):
        gs[q, 0:UNITS, :] = g_ref[:, q * QUARTER : (q + 1) * QUARTER]

    pl.semaphore_wait(barrier, jnp.where(lone, len(peers), len(peers) + 1))

    for n, xt in enumerate((xr, xl, xo)):
        send(("a", n), gs.at[xt], ga.at[x], dev(x=xt))
    ga[x] = gs[x]

    row = lax.broadcasted_iota(jnp.int32, (COLS, 8 * GROUP), 0)
    lane = lax.broadcasted_iota(jnp.int32, (COLS, 8 * GROUP), 1)
    place = row + 60 * ((row * 3277) >> 16)
    for part in range(3):
        total = None
        for q in range(NX):
            pick = jnp.where(lane == place + 20 * q, 1.0, 0.0).astype(BF16)
            start = q * (BLOCK // NX) + part * COLS
            term = dot(b_ref[start : start + COLS, :], pick, ((0,), (0,)))
            total = term if total is None else total + term
        bb[x, :, part * 640 : (part + 1) * 640] = total.astype(BF16)
    for h in range(2):
        rows = pl.ds(h * HALF, HALF)
        send(("b", "r", h), bb.at[x, rows], bb.at[x, rows], dev(x=xr))
        send(("b", "l", h), bb.at[x, rows], bb.at[x, rows], dev(x=xl))

    class Item:
        def __init__(self, name, ref, both, far):
            self.name, self.ref, self.both, self.far = name, ref, both, far

        def at(self, mine, shift):
            col = yl if mine else 1 - yl
            return self.ref(col * NZ + lax.rem(z + shift + 2 * NZ, NZ))

        def hop(self, way, mine, k, shift):
            ref = self.at(mine, shift)
            send((self.name, way, mine, k), ref, ref, right if way == "r" else left)

        def across(self, shift):
            ref = self.at(True, shift)
            send((self.name, "y", shift), ref, ref, pair_y)

        def last(self, way, mine):
            return 6 if (way == self.far) == mine else 5

        def begin(self):
            self.hop("r", True, 1, 0)
            self.hop("l", True, 1, 0)
            self.across(0)

        def begin_other(self):
            if self.both:
                got((self.name, "y", 0), self.at(False, 0))
                self.hop("r", False, 1, 0)
                self.hop("l", False, 1, 0)

        def step(self, k):
            for mine in (True, False) if self.both else (True,):
                for way, sign in (("r", -1), ("l", 1)):
                    if k <= self.last(way, mine):
                        got((self.name, way, mine, k), self.at(mine, sign * k))
                        if k < self.last(way, mine):
                            self.hop(way, mine, k + 1, sign * k)
                        if not self.both:
                            self.across(sign * k)

        def end(self):
            if not self.both:
                shifts = [0]
                for k in range(1, 7):
                    shifts += [s * k for w, s in (("r", -1), ("l", 1)) if k <= self.last(w, True)]
                for shift in shifts:
                    got((self.name, "y", shift), self.at(False, shift))

    grads = [
        Item("g0", lambda s: gb.at[0, s], False, "r"),
        Item("g1", lambda s: gb.at[1, s], True, "r"),
    ]
    rot = Item("r", lambda s: rb.at[s], False, "l")

    for n, xt in enumerate((xl, xr, xo)):
        got(("a", n), ga.at[xt])
    prow = lax.broadcasted_iota(jnp.int32, (GROUP, NX * 32), 0)
    plane = lax.broadcasted_iota(jnp.int32, (GROUP, NX * 32), 1)
    unit = plane & 31
    hit = jnp.logical_and(prow == (plane >> 5) * UNITS + unit, unit < UNITS)
    pick = jnp.where(hit, 1.0, 0.0).astype(BF16)
    packed = dot(pick, ga[...].reshape(NX * 32, QUARTER)).astype(BF16)
    for ch in range(CHUNKS):
        gb[ch, slot] = packed[:, ch * TW : (ch + 1) * TW]
        grads[ch].begin()

    load_bi.wait()
    load_in.wait()

    def slab(i, total):
        at = pl.ds(pl.multiple_of(i * 1536, 1536), 1536)
        return total + dot(iv[:, at], biv[at, :])

    tile = lax.fori_loop(0, DEPTH // 1536, slab, jnp.zeros((TOK, FEATS), F32))
    token = lax.broadcasted_iota(jnp.int32, (TOK, FEATS), 0)
    live = jnp.where(token < SLOT, cnt_ref[0], cnt_ref[1])
    tile = jnp.where((token & (SLOT - 1)) < live, tile, 0.0)
    rt[...] = tile.T.astype(BF16)
    own_copy = pltpu.make_async_copy(rt, rb.at[slot], lsem.at[2])

    swap_copy = copy(("swap",), rt, rb.at[c * NZ + z], swap)

    @pl.when(lone)
    def _():
        own_copy.start()
        own_copy.wait()

    @pl.when(jnp.logical_not(lone))
    def _():
        swap_copy.start()

    grads[1].begin_other()

    def rot_begin():
        @pl.when(jnp.logical_not(lone))
        def _():
            got(("swap",), rb.at[slot])

        rot.begin()

    for it in range(1, 9):
        for item in grads:
            if it <= 6:
                item.step(it)
        if it == 1:
            rot_begin()
        if 2 <= it <= 7:
            rot.step(it - 1)
        if it == 4:
            top = pl.ds(0, HALF)
            got(("b", "r", 0), bb.at[xl, top])
            send(("b", "rr"), bb.at[xl, top], bb.at[xl, top], dev(x=xr))
            got(("b", "l", 0), bb.at[xr, top])
            low = pl.ds(HALF, HALF)
            got(("b", "l", 1), bb.at[xr, low])
            send(("b", "ll"), bb.at[xr, low], bb.at[xr, low], dev(x=xl))
            got(("b", "r", 1), bb.at[xl, low])
    grads[0].end()
    got(("b", "rr"), bb.at[xo, pl.ds(0, HALF)])
    got(("b", "ll"), bb.at[xo, pl.ds(HALF, HALF)])

    def multiply(ch):
        weights = gb[ch].reshape(BLOCK, TW)
        for q in range(NX):
            part = dot(bb[q], weights)
            cb[ch, 0, q] = part[:HALF]
            cb[ch, 1, q] = part[HALF:]
        send(("c", ch), cb.at[ch, 1 - c], cr.at[ch], pair_c)

    def scatter(ch):
        got(("c", ch), cr.at[ch])
        for q in range(NX):
            ss[ch, q] = (cb[ch, c, q] + cr[ch, q]).astype(BF16)
        for r in (1, 2, 3):
            send(("s", ch, r), ss.at[ch, yhs[r]], sr.at[ch, r - 1], dev(yh=yhs[r]))

    def spread(ch):
        total = cb[ch, c, yh] + cr[ch, yh]
        for r in (1, 2, 3):
            got(("s", ch, r), sr.at[ch, r - 1])
            total = total + sr[ch, r - 1].astype(F32)
        ab[ch, yh, c] = total.astype(BF16)
        mine = ab.at[ch, yh, c]
        for r in (1, 2, 3):
            send(("t", ch, r), mine, mine, dev(yh=yhs[r]))
        send(("u", ch, 0), mine, mine, pair_c)

    def collect(ch):
        for r in (1, 3, 2):
            ref = ab.at[ch, yhs[NH - r], c]
            got(("t", ch, r), ref)
            send(("u", ch, r), ref, ref, pair_c)
        for r in range(NH):
            got(("u", ch, r), ab.at[ch, yhs[(NH - r) % NH], 1 - c])

    def products(ch, xt):
        for h in range(2):
            for f in range(3):
                total = None
                for e in range(TW // SLOT):
                    at = slice(e * SLOT, (e + 1) * SLOT)
                    first = ch * NZ + f * 4
                    rows = rb[first : first + 4, :, at].reshape(4 * FEATS, SLOT)
                    term = dot(ab[ch, xt, h, :, at], rows, ((1,), (1,)))
                    total = term * term if total is None else total + term * term
                where = (xt, pl.ds(h * HALF, HALF), pl.ds(f * 256, 256))
                acc[where] = total if ch == 0 else acc[where] + total

    for ch in range(CHUNKS):
        multiply(ch)
    for ch in range(CHUNKS):
        scatter(ch)
    for ch in range(CHUNKS):
        spread(ch)
    rot.end()
    collect(0)
    for xt in (xo, xr, xl, x):
        products(0, xt)
    collect(1)

    top, low = pl.ds(0, HALF), pl.ds(HALF, HALF)
    products(1, xo)
    o1s[0] = acc[xo, top].astype(BF16)
    send(("o1", "r"), o1s.at[0], o1r.at[0], dev(x=xr))
    o1s[1] = acc[xo, low].astype(BF16)
    send(("o1", "l"), o1s.at[1], o1r.at[1], dev(x=xl))
    products(1, xr)
    o2s[0, 1] = acc[xr, low].astype(BF16)
    send(("o2", "r", 1), o2s.at[0, 1], o2r.at[0, 1], dev(x=xr))
    products(1, xl)
    o2s[1, 0] = acc[xl, top].astype(BF16)
    send(("o2", "l", 0), o2s.at[1, 0], o2r.at[1, 0], dev(x=xl))
    got(("o1", "r"), o1r.at[0])
    o2s[0, 0] = (acc[xr, top] + o1r[0].astype(F32)).astype(BF16)
    send(("o2", "r", 0), o2s.at[0, 0], o2r.at[0, 0], dev(x=xr))
    got(("o1", "l"), o1r.at[1])
    o2s[1, 1] = (acc[xl, low] + o1r[1].astype(F32)).astype(BF16)
    send(("o2", "l", 1), o2s.at[1, 1], o2r.at[1, 1], dev(x=xl))
    products(1, x)
    for w, way in ((0, "r"), (1, "l")):
        for h in (1 - w, w):
            got(("o2", way, h), o2r.at[w, h])
    for h in range(2):
        rows = pl.ds(h * HALF, HALF)
        total = acc[x, rows] + o2r[0, h].astype(F32) + o2r[1, h].astype(F32)
        out_ref[rows, :] = total * FACTOR

    for cp in sent:
        cp.wait_send()

    @pl.when(jnp.logical_not(lone))
    def _():
        swap_copy.wait_send()

    assert len(keys) <= NSEM


def shards(out_grads, inputs, basis_grads, basis_inputs, counts):
    vmem = pl.BlockSpec(memory_space=pltpu.VMEM)
    hbm = pl.BlockSpec(memory_space=pl.ANY)
    return pl.pallas_call(
        kernel,
        out_shape=jax.ShapeDtypeStruct((COLS, WIDE), F32),
        in_specs=[vmem, vmem, hbm, hbm, pl.BlockSpec(memory_space=pltpu.SMEM)],
        out_specs=vmem,
        scratch_shapes=[
            pltpu.VMEM((NX, 32, QUARTER), BF16),
            pltpu.VMEM((NX, 32, QUARTER), BF16),
            pltpu.VMEM((CHUNKS, SLOTS, GROUP, TW), BF16),
            pltpu.VMEM((NX, COLS, BLOCK), BF16),
            pltpu.VMEM((TOK, DEPTH), BF16),
            pltpu.VMEM((DEPTH, FEATS), BF16),
            pltpu.VMEM((FEATS, TOK), BF16),
            pltpu.VMEM((SLOTS, FEATS, TOK), BF16),
            pltpu.VMEM((CHUNKS, 2, NX, HALF, TW), F32),
            pltpu.VMEM((CHUNKS, NX, HALF, TW), F32),
            pltpu.VMEM((CHUNKS, NX, HALF, TW), BF16),
            pltpu.VMEM((CHUNKS, 3, HALF, TW), BF16),
            pltpu.VMEM((CHUNKS, NH, NC, HALF, TW), BF16),
            pltpu.VMEM((NX, COLS, WIDE), F32),
            pltpu.VMEM((2, HALF, WIDE), BF16),
            pltpu.VMEM((2, HALF, WIDE), BF16),
            pltpu.VMEM((2, 2, HALF, WIDE), BF16),
            pltpu.VMEM((2, 2, HALF, WIDE), BF16),
            pltpu.SemaphoreType.DMA((NSEM,)),
            pltpu.SemaphoreType.DMA((NSEM,)),
            pltpu.SemaphoreType.DMA((4,)),
        ],
        compiler_params=pltpu.CompilerParams(
            collective_id=0, has_side_effects=True, vmem_limit_bytes=40 * 1024 * 1024
        ),
        cost_estimate=pl.CostEstimate(
            flops=2_200_000_000, bytes_accessed=10_000_000, transcendentals=0
        ),
    )(out_grads, basis_grads, inputs, basis_inputs, counts)


def solution(mesh):
    placed = (P(("dp", "basis"), None), P("dp", None), P("dp", "basis"), P(None, "basis"), P("dp"))
    return jax.shard_map(
        shards, mesh=mesh, in_specs=placed, out_specs=P("basis", "dp"), check_vma=False
    )
```

time: 1050 us -> 93.6 us (0.09)
  waiting for transfers between devices: 1000 us -> 0 us
  Pallas kernels: 0 us -> 85.7 us
  matrix products: 14.9 us -> 0 us
  between operations: 13.1 us -> 0.05 us
    all_gather x2 -> x0, waiting for transfers between devices: 836 us -> none  [the longest x1 425 us: shards(): wide_inputs = lax.all_gather(rotated_inputs, 'basis', axis=0, tiled=True)]
    reduce_scatter x2 -> x0, waiting for transfers between devices: 164 us -> none  [the longest x1 103 us: shards(): lax.psum_scatter(partial_value, 'dp', scatter_dimension=1, tiled=True)]
    pallas_call x0 -> x1, Pallas kernels: none -> 85.7 us  [shards(): pl.pallas_call(kernel, out_shape=jax.ShapeDtypeStruct((COLS, WIDE), F32),...]
    dot_general x3 -> x0, matrix products: 14.9 us -> none  [the longest x1 5.83 us: shards(): lax.dot_general(basis_grads, lax.all_gather(out_grads, 'basis', axis=0, t...]
  transfers between devices with their start and end apart: 4 -> 0, of which waited for: 4 -> 0; matrix products, arithmetic and copies ran while one was open for 2% -> 0% of each run, Pallas kernels for 0% -> 0%
where the time goes in v1:
time: 93.6 us; the launch traced here: 92 us
  Pallas kernels  85.7 us (92%)
  local copies, waits for them, and re-layouts  6.24 us (7%)
    pallas_call x1, Pallas kernels, shards(): pl.pallas_call(kernel, out_shape=jax.ShapeDtypeStruct((COLS, WIDE), F32),...  85.7 us
    unnamed x9, local copies, waits for them, and re-layouts  6.24 us

profile of v1, /device:TPU:1, one launch (start us, length us, event | category | flops | bytes accessed | tf_op | source)
XLA Modules:
  0.0 92.0 jit_solution(12035307518332590569)
XLA Ops:
  0.0 0.0 copy-start.2
  0.0 0.0 copy-start.1
  0.0 1.8 %copy.6.b_ref = bf16[1920,160]{1,0:T(8,128)(2,1)S(1)} copy(bf16[1920,160]{0,1:T(8,128)(2,1)} %param.7) | data formatting | bytes 1228800 | tf_op args[2]
  1.8 1.8 %copy.7.bi_ref = bf16[6144,64]{1,0:T(8,128)(2,1)S(1)} copy(bf16[6144,64]{0,1:T(8,128)(2,1)} %param.8) | data formatting | bytes 1572864 | tf_op args[3]
  3.6 0.0 copy-done.2
  3.6 0.0 copy-done.1
  3.6 0.0 copy-start
  3.6 1.9 %copy-done = bf16[256,6144]{1,0:T(8,128)(2,1)S(1)} copy-done((bf16[256,6144]{1,0:T(8,128)(2,1)S(1)}, bf16[256,6144]{1,0:T(8,128)(2,1)}, u32[]{:S(2)}) %copy-start) | copy-done | bytes 3145752
  5.5 85.7 %shard_map.55 = f32[160,768]{1,0:T(8,128)S(1)} custom-call(bf16[20,2048]{1,0:T(8,128)(2,1)S(1)} %copy-done.1, bf16[1920,160]{1,0:T(8,128)(2,1)S(1)} %copy.6.b_ref, bf16[256,6144]{1,0:T(8,128)(2,1)S(1)} %copy-done, bf16[6144,64]{1,0:T(8,128)(2,1)S(1)} %copy.7.bi_ref, s32[2]{0:T(128)S(1)} %copy-done.2), custom_call_target="tpu_custom_call" | custom-call | flops 2200000000 | bytes 10000000 | tf_op jit(solution)/shard_map/pallas_call | solution.py:334
  91.2 0.8 copy.9
Async XLA Ops:
  0.0 3.6 %copy-start.2 = (s32[2]{0:T(128)S(1)}, s32[2]{0:T(128)}, u32[]{:S(2)}) copy-start(s32[2]{0:T(128)} %cnt_ref.1) | copy-start | bytes 28
  0.0 3.6 %copy-start.1 = (bf16[20,2048]{1,0:T(8,128)(2,1)S(1)}, bf16[20,2048]{1,0:T(8,128)(2,1)}, u32[]{:S(2)}) copy-start(bf16[20,2048]{1,0:T(8,128)(2,1)} %g_ref.1) | copy-start | bytes 245764
  3.6 1.9 %copy-start = (bf16[256,6144]{1,0:T(8,128)(2,1)S(1)}, bf16[256,6144]{1,0:T(8,128)(2,1)}, u32[]{:S(2)}) copy-start(bf16[256,6144]{1,0:T(8,128)(2,1)} %in_ref.1) | copy-start | bytes 9437188

commit v2 on v1

--- a/solution.py
+++ b/solution.py
@@ -24,7 +24,7 @@
 TOK = 256
 DEPTH = 6144
 FACTOR = 1.0 / 2048.0
-NSEM = 128
+NSEM = 160
 
 
 def dot(a, b, dims=((1,), (0,))):
@@ -33,7 +33,7 @@
 
 def kernel(
     g_ref, b_ref, in_ref, bi_ref, cnt_ref, out_ref,
-    gs, ga, gb, bb, iv, biv, rt, rb, cb, cr, ss, sr, ab, acc, o1s, o1r, o2s, o2r,
+    gv, gs, ga, gb, bb, bv, picks, iv, biv, rt, rb, cb, cr, ss, sr, ab, acc, o1s, o1r, o2s, o2r,
     ssem, rsem, lsem,
 ):
     d, b = lax.axis_index("dp"), lax.axis_index("basis")
@@ -54,7 +54,8 @@
 
     barrier = pltpu.get_barrier_semaphore()
     peers = [right, left, pair_y, pair_c]
-    peers += [dev(x=xr), dev(x=xl), dev(x=xo)] + [dev(yh=yhs[r]) for r in (1, 2, 3)]
+    peers += [dev(x=n, yl=m) for n in (xr, xl, xo) for m in (yl, 1 - yl)]
+    peers += [dev(yh=yhs[r]) for r in (1, 2, 3)]
     for peer in peers:
         pl.semaphore_signal(barrier, inc=1, device_id=peer, device_id_type=MESH)
 
@@ -82,34 +83,41 @@
 
     load_in = pltpu.make_async_copy(in_ref, iv, lsem.at[0])
     load_bi = pltpu.make_async_copy(bi_ref, biv, lsem.at[1])
-    load_in.start()
-    load_bi.start()
+    load_g = pltpu.make_async_copy(g_ref, gv, lsem.at[2])
+    load_b = pltpu.make_async_copy(b_ref, bv, lsem.at[3])
+    for load in (load_g, load_b, load_bi, load_in):
+        load.start()
 
     gs[...] = jnp.zeros_like(gs)
+    load_g.wait()
     for q in range(NX):
-        gs[q, 0:UNITS, :] = g_ref[:, q * QUARTER : (q + 1) * QUARTER]
+        gs[q, 0:UNITS, :] = gv[:, q * QUARTER : (q + 1) * QUARTER]
 
     pl.semaphore_wait(barrier, jnp.where(lone, len(peers), len(peers) + 1))
 
     for n, xt in enumerate((xr, xl, xo)):
-        send(("a", n), gs.at[xt], ga.at[x], dev(x=xt))
-    ga[x] = gs[x]
-
+        send(("a", n, 0), gs.at[xt], ga.at[0, x], dev(x=xt))
+        send(("a", n, 1), gs.at[xt], ga.at[1, x], dev(x=xt, yl=1 - yl))
+    send(("a", 3, 1), gs.at[x], ga.at[1, x], pair_y)
+    ga[0, x] = gs[x]
+
+    load_b.wait()
     row = lax.broadcasted_iota(jnp.int32, (COLS, 8 * GROUP), 0)
     lane = lax.broadcasted_iota(jnp.int32, (COLS, 8 * GROUP), 1)
     place = row + 60 * ((row * 3277) >> 16)
+    for q in range(NX):
+        picks[q] = jnp.where(lane == place + UNITS * q, 1.0, 0.0).astype(BF16)
     for part in range(3):
         total = None
         for q in range(NX):
-            pick = jnp.where(lane == place + 20 * q, 1.0, 0.0).astype(BF16)
             start = q * (BLOCK // NX) + part * COLS
-            term = dot(b_ref[start : start + COLS, :], pick, ((0,), (0,)))
+            term = dot(bv[:, start : start + COLS], picks[q])
             total = term if total is None else total + term
         bb[x, :, part * 640 : (part + 1) * 640] = total.astype(BF16)
     for h in range(2):
-        rows = pl.ds(h * HALF, HALF)
-        send(("b", "r", h), bb.at[x, rows], bb.at[x, rows], dev(x=xr))
-        send(("b", "l", h), bb.at[x, rows], bb.at[x, rows], dev(x=xl))
+        for way, half, xt in (("r", h, xr), ("l", 1 - h, xl)):
+            ref = bb.at[x, pl.ds(half * HALF, HALF)]
+            send(("b", way, half), ref, ref, dev(x=xt))
 
     class Item:
         def __init__(self, name, ref, both, far):
@@ -130,16 +138,10 @@
         def last(self, way, mine):
             return 6 if (way == self.far) == mine else 5
 
-        def begin(self):
-            self.hop("r", True, 1, 0)
-            self.hop("l", True, 1, 0)
-            self.across(0)
-
-        def begin_other(self):
-            if self.both:
-                got((self.name, "y", 0), self.at(False, 0))
-                self.hop("r", False, 1, 0)
-                self.hop("l", False, 1, 0)
+        def begin(self, mine):
+            if mine or self.both:
+                self.hop("r", mine, 1, 0)
+                self.hop("l", mine, 1, 0)
 
         def step(self, k):
             for mine in (True, False) if self.both else (True,):
@@ -153,7 +155,7 @@
 
         def end(self):
             if not self.both:
-                shifts = [0]
+                shifts = []
                 for k in range(1, 7):
                     shifts += [s * k for w, s in (("r", -1), ("l", 1)) if k <= self.last(w, True)]
                 for shift in shifts:
@@ -163,70 +165,78 @@
         Item("g0", lambda s: gb.at[0, s], False, "r"),
         Item("g1", lambda s: gb.at[1, s], True, "r"),
     ]
-    rot = Item("r", lambda s: rb.at[s], False, "l")
+    rot = Item("r", lambda s: rb.at[s], True, "l")
+
+    load_bi.wait()
+    load_in.wait()
+
+    def slab(i, total):
+        at = pl.ds(pl.multiple_of(i * 1536, 1536), 1536)
+        return total + dot(iv[:, at], biv[:, at], ((1,), (1,)))
+
+    tile = lax.fori_loop(0, DEPTH // 1536, slab, jnp.zeros((TOK, FEATS), F32))
+    token = lax.broadcasted_iota(jnp.int32, (TOK, FEATS), 0)
+    live = jnp.where(token < SLOT, cnt_ref[0], cnt_ref[1])
+    tile = jnp.where((token & (SLOT - 1)) < live, tile, 0.0)
+    rt[...] = tile.T.astype(BF16)
+    own_copy = pltpu.make_async_copy(rt, rb.at[slot], lsem.at[4])
+
+    swap_copy = copy(("swap",), rt, rb.at[c * NZ + z], swap)
+
+    @pl.when(lone)
+    def _():
+        own_copy.start()
+        own_copy.wait()
+
+    @pl.when(jnp.logical_not(lone))
+    def _():
+        swap_copy.start()
 
     for n, xt in enumerate((xl, xr, xo)):
-        got(("a", n), ga.at[xt])
+        got(("a", n, 0), ga.at[0, xt])
+        got(("a", n, 1), ga.at[1, xt])
+    got(("a", 3, 1), ga.at[1, x])
     prow = lax.broadcasted_iota(jnp.int32, (GROUP, NX * 32), 0)
     plane = lax.broadcasted_iota(jnp.int32, (GROUP, NX * 32), 1)
     unit = plane & 31
     hit = jnp.logical_and(prow == (plane >> 5) * UNITS + unit, unit < UNITS)
     pick = jnp.where(hit, 1.0, 0.0).astype(BF16)
-    packed = dot(pick, ga[...].reshape(NX * 32, QUARTER)).astype(BF16)
-    for ch in range(CHUNKS):
-        gb[ch, slot] = packed[:, ch * TW : (ch + 1) * TW]
-        grads[ch].begin()
-
-    load_bi.wait()
-    load_in.wait()
-
-    def slab(i, total):
-        at = pl.ds(pl.multiple_of(i * 1536, 1536), 1536)
-        return total + dot(iv[:, at], biv[at, :])
-
-    tile = lax.fori_loop(0, DEPTH // 1536, slab, jnp.zeros((TOK, FEATS), F32))
-    token = lax.broadcasted_iota(jnp.int32, (TOK, FEATS), 0)
-    live = jnp.where(token < SLOT, cnt_ref[0], cnt_ref[1])
-    tile = jnp.where((token & (SLOT - 1)) < live, tile, 0.0)
-    rt[...] = tile.T.astype(BF16)
-    own_copy = pltpu.make_async_copy(rt, rb.at[slot], lsem.at[2])
-
-    swap_copy = copy(("swap",), rt, rb.at[c * NZ + z], swap)
-
-    @pl.when(lone)
-    def _():
-        own_copy.start()
-        own_copy.wait()
-
-    @pl.when(jnp.logical_not(lone))
-    def _():
-        swap_copy.start()
-
-    grads[1].begin_other()
+    for side, where in ((0, slot), (1, (1 - yl) * NZ + z)):
+        packed = dot(pick, ga[side].reshape(NX * 32, QUARTER)).astype(BF16)
+        for ch in range(CHUNKS):
+            gb[ch, where] = packed[:, ch * TW : (ch + 1) * TW]
+            grads[ch].begin(side == 0)
+
 
     def rot_begin():
         @pl.when(jnp.logical_not(lone))
         def _():
             got(("swap",), rb.at[slot])
 
-        rot.begin()
-
-    for it in range(1, 9):
+        rot.begin(True)
+        rot.across(0)
+
+    def rot_other():
+        got(("r", "y", 0), rot.at(False, 0))
+        rot.begin(False)
+
+    top, low = pl.ds(0, HALF), pl.ds(HALF, HALF)
+    for it in range(1, 7):
         for item in grads:
-            if it <= 6:
-                item.step(it)
-        if it == 1:
+            item.step(it)
+        if it == 2:
             rot_begin()
-        if 2 <= it <= 7:
-            rot.step(it - 1)
-        if it == 4:
-            top = pl.ds(0, HALF)
+        if it == 3:
+            rot_other()
+        if it >= 4:
+            rot.step(it - 3)
+        if it == 3:
             got(("b", "r", 0), bb.at[xl, top])
             send(("b", "rr"), bb.at[xl, top], bb.at[xl, top], dev(x=xr))
-            got(("b", "l", 0), bb.at[xr, top])
-            low = pl.ds(HALF, HALF)
             got(("b", "l", 1), bb.at[xr, low])
             send(("b", "ll"), bb.at[xr, low], bb.at[xr, low], dev(x=xl))
+        if it == 5:
+            got(("b", "l", 0), bb.at[xr, top])
             got(("b", "r", 1), bb.at[xl, low])
     grads[0].end()
     got(("b", "rr"), bb.at[xo, pl.ds(0, HALF)])
@@ -281,17 +291,18 @@
 
     for ch in range(CHUNKS):
         multiply(ch)
+    rot.step(4)
     for ch in range(CHUNKS):
         scatter(ch)
+    rot.step(5)
     for ch in range(CHUNKS):
         spread(ch)
-    rot.end()
+    rot.step(6)
     collect(0)
     for xt in (xo, xr, xl, x):
         products(0, xt)
     collect(1)
 
-    top, low = pl.ds(0, HALF), pl.ds(HALF, HALF)
     products(1, xo)
     o1s[0] = acc[xo, top].astype(BF16)
     send(("o1", "r"), o1s.at[0], o1r.at[0], dev(x=xr))
@@ -334,15 +345,18 @@
     return pl.pallas_call(
         kernel,
         out_shape=jax.ShapeDtypeStruct((COLS, WIDE), F32),
-        in_specs=[vmem, vmem, hbm, hbm, pl.BlockSpec(memory_space=pltpu.SMEM)],
+        in_specs=[hbm, hbm, hbm, hbm, pl.BlockSpec(memory_space=pltpu.SMEM)],
         out_specs=vmem,
         scratch_shapes=[
+            pltpu.VMEM((UNITS, NX * QUARTER), BF16),
             pltpu.VMEM((NX, 32, QUARTER), BF16),
-            pltpu.VMEM((NX, 32, QUARTER), BF16),
+            pltpu.VMEM((2, NX, 32, QUARTER), BF16),
             pltpu.VMEM((CHUNKS, SLOTS, GROUP, TW), BF16),
             pltpu.VMEM((NX, COLS, BLOCK), BF16),
+            pltpu.VMEM((COLS, BLOCK), BF16),
+            pltpu.VMEM((NX, COLS, 8 * GROUP), BF16),
             pltpu.VMEM((TOK, DEPTH), BF16),
-            pltpu.VMEM((DEPTH, FEATS), BF16),
+            pltpu.VMEM((FEATS, DEPTH), BF16),
             pltpu.VMEM((FEATS, TOK), BF16),
             pltpu.VMEM((SLOTS, FEATS, TOK), BF16),
             pltpu.VMEM((CHUNKS, 2, NX, HALF, TW), F32),
@@ -357,15 +371,15 @@
             pltpu.VMEM((2, 2, HALF, WIDE), BF16),
             pltpu.SemaphoreType.DMA((NSEM,)),
             pltpu.SemaphoreType.DMA((NSEM,)),
-            pltpu.SemaphoreType.DMA((4,)),
+            pltpu.SemaphoreType.DMA((5,)),
         ],
         compiler_params=pltpu.CompilerParams(
-            collective_id=0, has_side_effects=True, vmem_limit_bytes=40 * 1024 * 1024
+            collective_id=0, has_side_effects=True, vmem_limit_bytes=56 * 1024 * 1024
         ),
         cost_estimate=pl.CostEstimate(
             flops=2_200_000_000, bytes_accessed=10_000_000, transcendentals=0
         ),
-    )(out_grads, basis_grads, inputs, basis_inputs, counts)
+    )(out_grads, basis_grads.T, inputs, basis_inputs.T, counts)
 
 
 def solution(mesh):

time: 93.6 us -> 88.6 us (0.947); the launches traced: 92 us -> 88.5 us
  local copies, waits for them, and re-layouts: 6.24 us -> 1.84 us
    unnamed x9 -> x1, local copies, waits for them, and re-layouts: 6.24 us -> 1.84 us
where the time goes in v2:
time: 88.6 us; the launch traced here: 88.5 us
  Pallas kernels  86.6 us (98%)
  local copies, waits for them, and re-layouts  1.84 us (2%)
    pallas_call x1, Pallas kernels, shards(): pl.pallas_call(kernel, out_shape=jax.ShapeDtypeStruct((COLS, WIDE), F32),...  86.6 us
    unnamed x1, local copies, waits for them, and re-layouts  1.84 us

profile of v2, /device:TPU:1, one launch (start us, length us, event | category | flops | bytes accessed | tf_op | source)
XLA Modules:
  0.0 88.5 jit_solution(17328023233138148101)
XLA Ops:
  0.0 86.6 %shard_map.55 = f32[160,768]{1,0:T(8,128)} custom-call(bf16[20,2048]{1,0:T(8,128)(2,1)} %g_ref.1, bf16[160,1920]{1,0:T(8,128)(2,1)} %bitcast.3, bf16[256,6144]{1,0:T(8,128)(2,1)} %in_ref.1, bf16[64,6144]{1,0:T(8,128)(2,1)} %bitcast.2, s32[2]{0:T(128)} %cnt_ref.1), custom_call_target="tpu_custom_call" | custom-call | flops 2200000000 | bytes 10000000 | tf_op jit(solution)/shard_map/pallas_call | solution.py:345
  86.6 1.8 %copy.7 = f32[160,768]{1,0:T(8,128)} copy(f32[160,768]{1,0:T(8,128)} %shard_map.55) | data formatting | bytes 983040

commit v3 on v2

--- a/solution.py
+++ b/solution.py
@@ -24,7 +24,7 @@
 TOK = 256
 DEPTH = 6144
 FACTOR = 1.0 / 2048.0
-NSEM = 160
+NSEM = 192
 
 
 def dot(a, b, dims=((1,), (0,))):
@@ -50,12 +50,15 @@
     pair_y, pair_c = dev(yl=1 - yl), dev(c=1 - c)
     right, left = dev(z=zr), dev(z=zl)
     swap = dev(yh=x, c=yl, x=yh, yl=c)
+    swap_to = dev(yh=x, c=yl, x=yh, yl=1 - c)
+    swap_from = dev(yh=x, c=1 - yl, x=yh, yl=c)
     lone = jnp.logical_and(yh == x, c == yl)
 
     barrier = pltpu.get_barrier_semaphore()
     peers = [right, left, pair_y, pair_c]
     peers += [dev(x=n, yl=m) for n in (xr, xl, xo) for m in (yl, 1 - yl)]
     peers += [dev(yh=yhs[r]) for r in (1, 2, 3)]
+    peers += [swap_from]
     for peer in peers:
         pl.semaphore_signal(barrier, inc=1, device_id=peer, device_id_type=MESH)
 
@@ -167,31 +170,6 @@
     ]
     rot = Item("r", lambda s: rb.at[s], True, "l")
 
-    load_bi.wait()
-    load_in.wait()
-
-    def slab(i, total):
-        at = pl.ds(pl.multiple_of(i * 1536, 1536), 1536)
-        return total + dot(iv[:, at], biv[:, at], ((1,), (1,)))
-
-    tile = lax.fori_loop(0, DEPTH // 1536, slab, jnp.zeros((TOK, FEATS), F32))
-    token = lax.broadcasted_iota(jnp.int32, (TOK, FEATS), 0)
-    live = jnp.where(token < SLOT, cnt_ref[0], cnt_ref[1])
-    tile = jnp.where((token & (SLOT - 1)) < live, tile, 0.0)
-    rt[...] = tile.T.astype(BF16)
-    own_copy = pltpu.make_async_copy(rt, rb.at[slot], lsem.at[4])
-
-    swap_copy = copy(("swap",), rt, rb.at[c * NZ + z], swap)
-
-    @pl.when(lone)
-    def _():
-        own_copy.start()
-        own_copy.wait()
-
-    @pl.when(jnp.logical_not(lone))
-    def _():
-        swap_copy.start()
-
     for n, xt in enumerate((xl, xr, xo)):
         got(("a", n, 0), ga.at[0, xt])
         got(("a", n, 1), ga.at[1, xt])
@@ -207,6 +185,32 @@
             gb[ch, where] = packed[:, ch * TW : (ch + 1) * TW]
             grads[ch].begin(side == 0)
 
+    load_bi.wait()
+    load_in.wait()
+
+    def slab(i, total):
+        at = pl.ds(pl.multiple_of(i * 1536, 1536), 1536)
+        return total + dot(iv[:, at], biv[:, at], ((1,), (1,)))
+
+    tile = lax.fori_loop(0, DEPTH // 1536, slab, jnp.zeros((TOK, FEATS), F32))
+    token = lax.broadcasted_iota(jnp.int32, (TOK, FEATS), 0)
+    live = jnp.where(token < SLOT, cnt_ref[0], cnt_ref[1])
+    tile = jnp.where((token & (SLOT - 1)) < live, tile, 0.0)
+    rt[...] = tile.T.astype(BF16)
+    own_copy = pltpu.make_async_copy(rt, rb.at[slot], lsem.at[4])
+
+    swap_copy = copy(("swap",), rt, rb.at[c * NZ + z], swap)
+
+    send(("swap", 2), rt, rb.at[c * NZ + z], swap_to)
+
+    @pl.when(lone)
+    def _():
+        own_copy.start()
+        own_copy.wait()
+
+    @pl.when(jnp.logical_not(lone))
+    def _():
+        swap_copy.start()
 
     def rot_begin():
         @pl.when(jnp.logical_not(lone))
@@ -214,20 +218,15 @@
             got(("swap",), rb.at[slot])
 
         rot.begin(True)
-        rot.across(0)
-
-    def rot_other():
-        got(("r", "y", 0), rot.at(False, 0))
+        got(("swap", 2), rot.at(False, 0))
         rot.begin(False)
 
     top, low = pl.ds(0, HALF), pl.ds(HALF, HALF)
     for it in range(1, 7):
         for item in grads:
             item.step(it)
-        if it == 2:
+        if it == 3:
             rot_begin()
-        if it == 3:
-            rot_other()
         if it >= 4:
             rot.step(it - 3)
         if it == 3:
@@ -242,91 +241,98 @@
     got(("b", "rr"), bb.at[xo, pl.ds(0, HALF)])
     got(("b", "ll"), bb.at[xo, pl.ds(HALF, HALF)])
 
-    def multiply(ch):
-        weights = gb[ch].reshape(BLOCK, TW)
-        for q in range(NX):
-            part = dot(bb[q], weights)
-            cb[ch, 0, q] = part[:HALF]
-            cb[ch, 1, q] = part[HALF:]
-        send(("c", ch), cb.at[ch, 1 - c], cr.at[ch], pair_c)
-
-    def scatter(ch):
-        got(("c", ch), cr.at[ch])
-        for q in range(NX):
-            ss[ch, q] = (cb[ch, c, q] + cr[ch, q]).astype(BF16)
-        for r in (1, 2, 3):
-            send(("s", ch, r), ss.at[ch, yhs[r]], sr.at[ch, r - 1], dev(yh=yhs[r]))
-
-    def spread(ch):
-        total = cb[ch, c, yh] + cr[ch, yh]
-        for r in (1, 2, 3):
-            got(("s", ch, r), sr.at[ch, r - 1])
-            total = total + sr[ch, r - 1].astype(F32)
-        ab[ch, yh, c] = total.astype(BF16)
-        mine = ab.at[ch, yh, c]
-        for r in (1, 2, 3):
-            send(("t", ch, r), mine, mine, dev(yh=yhs[r]))
-        send(("u", ch, 0), mine, mine, pair_c)
-
-    def collect(ch):
+    blocks = (xo, xr, xl, x)
+
+    def multiply(i):
+        for ch in range(CHUNKS):
+            part = dot(bb[blocks[i]], gb[ch].reshape(BLOCK, TW))
+            for e in range(TW // SLOT):
+                for h in range(2):
+                    at = slice(e * SLOT, (e + 1) * SLOT)
+                    cb[i, h, ch * (TW // SLOT) + e] = part[h * HALF : (h + 1) * HALF, at]
+        send(("c", i), cb.at[i, 1 - c], cr.at[i], pair_c)
+
+    def scatter(i):
+        got(("c", i), cr.at[i])
+        for e in range(NH):
+            ss[i, e] = (cb[i, c, e] + cr[i, e]).astype(BF16)
+        for r in (2, 1, 3):
+            send(("s", i, r), ss.at[i, yhs[r]], sr.at[i, r - 1], dev(yh=yhs[r]))
+
+    def spread(i):
+        total = cb[i, c, yh] + cr[i, yh]
         for r in (1, 3, 2):
-            ref = ab.at[ch, yhs[NH - r], c]
-            got(("t", ch, r), ref)
-            send(("u", ch, r), ref, ref, pair_c)
+            got(("s", i, r), sr.at[i, r - 1])
+            total = total + sr[i, r - 1].astype(F32)
+        ab[i, c, yh] = total.astype(BF16)
+        mine = ab.at[i, c, yh]
+        for r in (2, 1, 3):
+            send(("t", i, r), mine, mine, dev(yh=yhs[r]))
+        send(("u", i, 0), mine, mine, pair_c)
+
+    def collect(i):
+        for r in (1, 3, 2):
+            ref = ab.at[i, c, yhs[NH - r]]
+            got(("t", i, r), ref)
+            send(("u", i, r), ref, ref, pair_c)
+
+    def products(i):
         for r in range(NH):
-            got(("u", ch, r), ab.at[ch, yhs[(NH - r) % NH], 1 - c])
-
-    def products(ch, xt):
+            got(("u", i, r), ab.at[i, 1 - c, yhs[(NH - r) % NH]])
         for h in range(2):
             for f in range(3):
                 total = None
-                for e in range(TW // SLOT):
-                    at = slice(e * SLOT, (e + 1) * SLOT)
-                    first = ch * NZ + f * 4
+                for e in range(NH):
+                    first = (e // 2) * NZ + f * 4
+                    at = slice((e % 2) * SLOT, (e % 2 + 1) * SLOT)
                     rows = rb[first : first + 4, :, at].reshape(4 * FEATS, SLOT)
-                    term = dot(ab[ch, xt, h, :, at], rows, ((1,), (1,)))
+                    term = dot(ab[i, h, e], rows, ((1,), (1,)))
                     total = term * term if total is None else total + term * term
-                where = (xt, pl.ds(h * HALF, HALF), pl.ds(f * 256, 256))
-                acc[where] = total if ch == 0 else acc[where] + total
-
-    for ch in range(CHUNKS):
-        multiply(ch)
+                acc[i, pl.ds(h * HALF, HALF), pl.ds(f * 256, 256)] = total
+
+    multiply(0)
+    multiply(1)
+    scatter(0)
     rot.step(4)
-    for ch in range(CHUNKS):
-        scatter(ch)
+    multiply(2)
+    scatter(1)
+    multiply(3)
+    scatter(2)
+    spread(0)
     rot.step(5)
-    for ch in range(CHUNKS):
-        spread(ch)
+    scatter(3)
+    spread(1)
     rot.step(6)
     collect(0)
-    for xt in (xo, xr, xl, x):
-        products(0, xt)
+    spread(2)
+    products(0)
+    o1s[0] = acc[0, top].astype(BF16)
+    send(("o1", "r"), o1s.at[0], o1r.at[0], dev(x=xr))
+    o1s[1] = acc[0, low].astype(BF16)
+    send(("o1", "l"), o1s.at[1], o1r.at[1], dev(x=xl))
     collect(1)
-
-    products(1, xo)
-    o1s[0] = acc[xo, top].astype(BF16)
-    send(("o1", "r"), o1s.at[0], o1r.at[0], dev(x=xr))
-    o1s[1] = acc[xo, low].astype(BF16)
-    send(("o1", "l"), o1s.at[1], o1r.at[1], dev(x=xl))
-    products(1, xr)
-    o2s[0, 1] = acc[xr, low].astype(BF16)
+    spread(3)
+    products(1)
+    o2s[0, 1] = acc[1, low].astype(BF16)
     send(("o2", "r", 1), o2s.at[0, 1], o2r.at[0, 1], dev(x=xr))
-    products(1, xl)
-    o2s[1, 0] = acc[xl, top].astype(BF16)
+    collect(2)
+    products(2)
+    o2s[1, 0] = acc[2, top].astype(BF16)
     send(("o2", "l", 0), o2s.at[1, 0], o2r.at[1, 0], dev(x=xl))
     got(("o1", "r"), o1r.at[0])
-    o2s[0, 0] = (acc[xr, top] + o1r[0].astype(F32)).astype(BF16)
+    o2s[0, 0] = (acc[1, top] + o1r[0].astype(F32)).astype(BF16)
     send(("o2", "r", 0), o2s.at[0, 0], o2r.at[0, 0], dev(x=xr))
     got(("o1", "l"), o1r.at[1])
-    o2s[1, 1] = (acc[xl, low] + o1r[1].astype(F32)).astype(BF16)
+    o2s[1, 1] = (acc[2, low] + o1r[1].astype(F32)).astype(BF16)
     send(("o2", "l", 1), o2s.at[1, 1], o2r.at[1, 1], dev(x=xl))
-    products(1, x)
+    collect(3)
+    products(3)
     for w, way in ((0, "r"), (1, "l")):
         for h in (1 - w, w):
             got(("o2", way, h), o2r.at[w, h])
     for h in range(2):
         rows = pl.ds(h * HALF, HALF)
-        total = acc[x, rows] + o2r[0, h].astype(F32) + o2r[1, h].astype(F32)
+        total = acc[3, rows] + o2r[0, h].astype(F32) + o2r[1, h].astype(F32)
         out_ref[rows, :] = total * FACTOR
 
     for cp in sent:
@@ -359,11 +365,11 @@
             pltpu.VMEM((FEATS, DEPTH), BF16),
             pltpu.VMEM((FEATS, TOK), BF16),
             pltpu.VMEM((SLOTS, FEATS, TOK), BF16),
-            pltpu.VMEM((CHUNKS, 2, NX, HALF, TW), F32),
-            pltpu.VMEM((CHUNKS, NX, HALF, TW), F32),
-            pltpu.VMEM((CHUNKS, NX, HALF, TW), BF16),
-            pltpu.VMEM((CHUNKS, 3, HALF, TW), BF16),
-            pltpu.VMEM((CHUNKS, NH, NC, HALF, TW), BF16),
+            pltpu.VMEM((NX, NC, NH, HALF, SLOT), F32),
+            pltpu.VMEM((NX, NH, HALF, SLOT), F32),
+            pltpu.VMEM((NX, NH, HALF, SLOT), BF16),
+            pltpu.VMEM((NX, 3, HALF, SLOT), BF16),
+            pltpu.VMEM((NX, NC, NH, HALF, SLOT), BF16),
             pltpu.VMEM((NX, COLS, WIDE), F32),
             pltpu.VMEM((2, HALF, WIDE), BF16),
             pltpu.VMEM((2, HALF, WIDE), BF16),

time: 88.6 us -> 82.7 us (0.933)
  Pallas kernels: 86.6 us -> 80.7 us
    pallas_call x1, Pallas kernels: 86.6 us -> 80.7 us  [shards(): pl.pallas_call(kernel, out_shape=jax.ShapeDtypeStruct((COLS, WIDE), F32),...]
where the time goes in v3:
time: 82.7 us; the launch traced here: 82.5 us
  Pallas kernels  80.7 us (98%)
  local copies, waits for them, and re-layouts  1.84 us (2%)
    pallas_call x1, Pallas kernels, shards(): pl.pallas_call(kernel, out_shape=jax.ShapeDtypeStruct((COLS, WIDE), F32),...  80.7 us
    unnamed x1, local copies, waits for them, and re-layouts  1.84 us

profile of v3, /device:TPU:1, one launch (start us, length us, event | category | flops | bytes accessed | tf_op | source)
XLA Modules:
  0.0 82.5 jit_solution(11917743170011830379)
XLA Ops:
  0.0 80.7 %shard_map.55 = f32[160,768]{1,0:T(8,128)} custom-call(bf16[20,2048]{1,0:T(8,128)(2,1)} %g_ref.1, bf16[160,1920]{1,0:T(8,128)(2,1)} %bitcast.3, bf16[256,6144]{1,0:T(8,128)(2,1)} %in_ref.1, bf16[64,6144]{1,0:T(8,128)(2,1)} %bitcast.2, s32[2]{0:T(128)} %cnt_ref.1), custom_call_target="tpu_custom_call" | custom-call | flops 2200000000 | bytes 10000000 | tf_op jit(solution)/shard_map/pallas_call | solution.py:351
  80.7 1.8 %copy.7 = f32[160,768]{1,0:T(8,128)} copy(f32[160,768]{1,0:T(8,128)} %shard_map.55) | data formatting | bytes 983040

commit v4 on v3

--- a/solution.py
+++ b/solution.py
@@ -16,15 +16,16 @@
 COLS = 160
 HALF = COLS // 2
 QUARTER = 512
-CHUNKS = 2
+CHUNKS = 4
 TW = QUARTER // CHUNKS
+PAIR = 2 * TW
 SLOT = 128
 FEATS = 64
 WIDE = NZ * FEATS
 TOK = 256
 DEPTH = 6144
 FACTOR = 1.0 / 2048.0
-NSEM = 192
+NSEM = 256
 
 
 def dot(a, b, dims=((1,), (0,))):
@@ -33,7 +34,7 @@
 
 def kernel(
     g_ref, b_ref, in_ref, bi_ref, cnt_ref, out_ref,
-    gv, gs, ga, gb, bb, bv, picks, iv, biv, rt, rb, cb, cr, ss, sr, ab, acc, o1s, o1r, o2s, o2r,
+    gv, gs, ga, go, gb, bb, bv, picks, iv, biv, rt, rb, cb, cr, ss, sr, ab, acc, o1s, o1r, o2s, o2r,
     ssem, rsem, lsem,
 ):
     d, b = lax.axis_index("dp"), lax.axis_index("basis")
@@ -94,15 +95,17 @@
     gs[...] = jnp.zeros_like(gs)
     load_g.wait()
     for q in range(NX):
-        gs[q, 0:UNITS, :] = gv[:, q * QUARTER : (q + 1) * QUARTER]
+        for h in range(2):
+            start = q * QUARTER + h * PAIR
+            gs[q, h, 0:UNITS, :] = gv[:, start : start + PAIR]
 
     pl.semaphore_wait(barrier, jnp.where(lone, len(peers), len(peers) + 1))
 
     for n, xt in enumerate((xr, xl, xo)):
-        send(("a", n, 0), gs.at[xt], ga.at[0, x], dev(x=xt))
-        send(("a", n, 1), gs.at[xt], ga.at[1, x], dev(x=xt, yl=1 - yl))
-    send(("a", 3, 1), gs.at[x], ga.at[1, x], pair_y)
-    ga[0, x] = gs[x]
+        send(("a", n, 0), gs.at[xt], ga.at[x], dev(x=xt))
+        send(("a", n, 1), gs.at[xt, 1], go.at[x], dev(x=xt, yl=1 - yl))
+    send(("a", 3, 1), gs.at[x, 1], go.at[x], pair_y)
+    ga[x] = gs[x]
 
     load_b.wait()
     row = lax.broadcasted_iota(jnp.int32, (COLS, 8 * GROUP), 0)
@@ -158,7 +161,7 @@
 
         def end(self):
             if not self.both:
-                shifts = []
+                shifts = [0]
                 for k in range(1, 7):
                     shifts += [s * k for w, s in (("r", -1), ("l", 1)) if k <= self.last(w, True)]
                 for shift in shifts:
@@ -166,24 +169,32 @@
 
     grads = [
         Item("g0", lambda s: gb.at[0, s], False, "r"),
-        Item("g1", lambda s: gb.at[1, s], True, "r"),
+        Item("g1", lambda s: gb.at[1, s], False, "l"),
+        Item("g2", lambda s: gb.at[2, s], True, "r"),
+        Item("g3", lambda s: gb.at[3, s], True, "l"),
     ]
     rot = Item("r", lambda s: rb.at[s], True, "l")
 
     for n, xt in enumerate((xl, xr, xo)):
-        got(("a", n, 0), ga.at[0, xt])
-        got(("a", n, 1), ga.at[1, xt])
-    got(("a", 3, 1), ga.at[1, x])
+        got(("a", n, 0), ga.at[xt])
     prow = lax.broadcasted_iota(jnp.int32, (GROUP, NX * 32), 0)
     plane = lax.broadcasted_iota(jnp.int32, (GROUP, NX * 32), 1)
     unit = plane & 31
     hit = jnp.logical_and(prow == (plane >> 5) * UNITS + unit, unit < UNITS)
     pick = jnp.where(hit, 1.0, 0.0).astype(BF16)
-    for side, where in ((0, slot), (1, (1 - yl) * NZ + z)):
-        packed = dot(pick, ga[side].reshape(NX * 32, QUARTER)).astype(BF16)
-        for ch in range(CHUNKS):
-            gb[ch, where] = packed[:, ch * TW : (ch + 1) * TW]
-            grads[ch].begin(side == 0)
+    for h in range(2):
+        packed = dot(pick, ga[:, h].reshape(NX * 32, PAIR)).astype(BF16)
+        for ch in (2 * h, 2 * h + 1):
+            gb[ch, slot] = packed[:, (ch % 2) * TW : (ch % 2 + 1) * TW]
+            grads[ch].begin(True)
+            if not grads[ch].both:
+                grads[ch].across(0)
+    for n, xt in enumerate((xl, xr, xo, x)):
+        got(("a", n, 1), go.at[xt])
+    packed = dot(pick, go[...].reshape(NX * 32, PAIR)).astype(BF16)
+    for ch in (2, 3):
+        gb[ch, (1 - yl) * NZ + z] = packed[:, (ch % 2) * TW : (ch % 2 + 1) * TW]
+        grads[ch].begin(False)
 
     load_bi.wait()
     load_in.wait()
@@ -225,10 +236,10 @@
     for it in range(1, 7):
         for item in grads:
             item.step(it)
-        if it == 3:
+        if it == 4:
             rot_begin()
-        if it >= 4:
-            rot.step(it - 3)
+        if it >= 5:
+            rot.step(it - 4)
         if it == 3:
             got(("b", "r", 0), bb.at[xl, top])
             send(("b", "rr"), bb.at[xl, top], bb.at[xl, top], dev(x=xr))
@@ -238,18 +249,20 @@
             got(("b", "l", 0), bb.at[xr, top])
             got(("b", "r", 1), bb.at[xl, low])
     grads[0].end()
+    grads[1].end()
     got(("b", "rr"), bb.at[xo, pl.ds(0, HALF)])
     got(("b", "ll"), bb.at[xo, pl.ds(HALF, HALF)])
 
     blocks = (xo, xr, xl, x)
 
     def multiply(i):
-        for ch in range(CHUNKS):
-            part = dot(bb[blocks[i]], gb[ch].reshape(BLOCK, TW))
-            for e in range(TW // SLOT):
+        for ch in range(0, CHUNKS, 2):
+            both = [gb[ch + e].reshape(BLOCK, TW) for e in range(2)]
+            part = dot(bb[blocks[i]], jnp.concatenate(both, axis=1))
+            for e in range(2):
                 for h in range(2):
                     at = slice(e * SLOT, (e + 1) * SLOT)
-                    cb[i, h, ch * (TW // SLOT) + e] = part[h * HALF : (h + 1) * HALF, at]
+                    cb[i, h, ch + e] = part[h * HALF : (h + 1) * HALF, at]
         send(("c", i), cb.at[i, 1 - c], cr.at[i], pair_c)
 
     def scatter(i):
@@ -293,18 +306,19 @@
     multiply(0)
     multiply(1)
     scatter(0)
-    rot.step(4)
+    rot.step(3)
     multiply(2)
     scatter(1)
     multiply(3)
     scatter(2)
     spread(0)
-    rot.step(5)
+    rot.step(4)
     scatter(3)
     spread(1)
-    rot.step(6)
+    rot.step(5)
     collect(0)
     spread(2)
+    rot.step(6)
     products(0)
     o1s[0] = acc[0, top].astype(BF16)
     send(("o1", "r"), o1s.at[0], o1r.at[0], dev(x=xr))
@@ -355,8 +369,9 @@
         out_specs=vmem,
         scratch_shapes=[
             pltpu.VMEM((UNITS, NX * QUARTER), BF16),
-            pltpu.VMEM((NX, 32, QUARTER), BF16),
-            pltpu.VMEM((2, NX, 32, QUARTER), BF16),
+            pltpu.VMEM((NX, 2, 32, PAIR), BF16),
+            pltpu.VMEM((NX, 2, 32, PAIR), BF16),
+            pltpu.VMEM((NX, 32, PAIR), BF16),
             pltpu.VMEM((CHUNKS, SLOTS, GROUP, TW), BF16),
             pltpu.VMEM((NX, COLS, BLOCK), BF16),
             pltpu.VMEM((COLS, BLOCK), BF16),

time: 82.7 us -> 82.6 us (level)
  no operation moved by 1% of the time
where the time goes in v4:
time: 82.6 us; the launch traced here: 82.2 us
  Pallas kernels  80.4 us (97%)
  local copies, waits for them, and re-layouts  1.84 us (2%)
    pallas_call x1, Pallas kernels, shards(): pl.pallas_call(kernel, out_shape=jax.ShapeDtypeStruct((COLS, WIDE), F32),...  80.4 us
    unnamed x1, local copies, waits for them, and re-layouts  1.84 us

profile of v4, /device:TPU:1, one launch (start us, length us, event | category | flops | bytes accessed | tf_op | source)
XLA Modules:
  0.0 82.2 jit_solution(915220531128549483)
XLA Ops:
  0.0 80.4 %shard_map.55 = f32[160,768]{1,0:T(8,128)} custom-call(bf16[20,2048]{1,0:T(8,128)(2,1)} %g_ref.1, bf16[160,1920]{1,0:T(8,128)(2,1)} %bitcast.3, bf16[256,6144]{1,0:T(8,128)(2,1)} %in_ref.1, bf16[64,6144]{1,0:T(8,128)(2,1)} %bitcast.2, s32[2]{0:T(128)} %cnt_ref.1), custom_call_target="tpu_custom_call" | custom-call | flops 2200000000 | bytes 10000000 | tf_op jit(solution)/shard_map/pallas_call | solution.py:365
  80.4 1.8 %copy.7 = f32[160,768]{1,0:T(8,128)} copy(f32[160,768]{1,0:T(8,128)} %shard_map.55) | data formatting | bytes 983040

commit v5 on v4

--- a/solution.py
+++ b/solution.py
@@ -34,7 +34,7 @@
 
 def kernel(
     g_ref, b_ref, in_ref, bi_ref, cnt_ref, out_ref,
-    gv, gs, ga, go, gb, bb, bv, picks, iv, biv, rt, rb, cb, cr, ss, sr, ab, acc, o1s, o1r, o2s, o2r,
+    gs, ga, go, gb, bb, bv, picks, iv, biv, rt, rb, cb, cr, ss, sr, ab, acc, o1s, o1r, o2s, o2r,
     ssem, rsem, lsem,
 ):
     d, b = lax.axis_index("dp"), lax.axis_index("basis")
@@ -87,17 +87,15 @@
 
     load_in = pltpu.make_async_copy(in_ref, iv, lsem.at[0])
     load_bi = pltpu.make_async_copy(bi_ref, biv, lsem.at[1])
-    load_g = pltpu.make_async_copy(g_ref, gv, lsem.at[2])
     load_b = pltpu.make_async_copy(b_ref, bv, lsem.at[3])
-    for load in (load_g, load_b, load_bi, load_in):
+    for load in (load_b, load_bi, load_in):
         load.start()
 
     gs[...] = jnp.zeros_like(gs)
-    load_g.wait()
     for q in range(NX):
         for h in range(2):
             start = q * QUARTER + h * PAIR
-            gs[q, h, 0:UNITS, :] = gv[:, start : start + PAIR]
+            gs[q, h, 0:UNITS, :] = g_ref[:, start : start + PAIR]
 
     pl.semaphore_wait(barrier, jnp.where(lone, len(peers), len(peers) + 1))
 
@@ -158,14 +156,17 @@
                             self.hop(way, mine, k + 1, sign * k)
                         if not self.both:
                             self.across(sign * k)
+            if not self.both and k >= 2:
+                self.crossed(k - 2)
+
+        def crossed(self, k):
+            ways = [(w, g) for w, g in (("r", -1), ("l", 1)) if k <= self.last(w, True)]
+            for shift in [g * k for w, g in ways] if k else [0]:
+                got((self.name, "y", shift), self.at(False, shift))
 
         def end(self):
-            if not self.both:
-                shifts = [0]
-                for k in range(1, 7):
-                    shifts += [s * k for w, s in (("r", -1), ("l", 1)) if k <= self.last(w, True)]
-                for shift in shifts:
-                    got((self.name, "y", shift), self.at(False, shift))
+            self.crossed(5)
+            self.crossed(6)
 
     grads = [
         Item("g0", lambda s: gb.at[0, s], False, "r"),
@@ -174,6 +175,33 @@
         Item("g3", lambda s: gb.at[3, s], True, "l"),
     ]
     rot = Item("r", lambda s: rb.at[s], True, "l")
+
+    load_bi.wait()
+    load_in.wait()
+
+    def slab(i, total):
+        at = pl.ds(pl.multiple_of(i * 1536, 1536), 1536)
+        return total + dot(iv[:, at], biv[:, at], ((1,), (1,)))
+
+    tile = lax.fori_loop(0, DEPTH // 1536, slab, jnp.zeros((TOK, FEATS), F32))
+    token = lax.broadcasted_iota(jnp.int32, (TOK, FEATS), 0)
+    live = jnp.where(token < SLOT, cnt_ref[0], cnt_ref[1])
+    tile = jnp.where((token & (SLOT - 1)) < live, tile, 0.0)
+    rt[...] = tile.T.astype(BF16)
+    own_copy = pltpu.make_async_copy(rt, rb.at[slot], lsem.at[4])
+
+    swap_copy = copy(("swap",), rt, rb.at[c * NZ + z], swap)
+
+    send(("swap", 2), rt, rb.at[c * NZ + z], swap_to)
+
+    @pl.when(lone)
+    def _():
+        own_copy.start()
+        own_copy.wait()
+
+    @pl.when(jnp.logical_not(lone))
+    def _():
+        swap_copy.start()
 
     for n, xt in enumerate((xl, xr, xo)):
         got(("a", n, 0), ga.at[xt])
@@ -196,33 +224,6 @@
         gb[ch, (1 - yl) * NZ + z] = packed[:, (ch % 2) * TW : (ch % 2 + 1) * TW]
         grads[ch].begin(False)
 
-    load_bi.wait()
-    load_in.wait()
-
-    def slab(i, total):
-        at = pl.ds(pl.multiple_of(i * 1536, 1536), 1536)
-        return total + dot(iv[:, at], biv[:, at], ((1,), (1,)))
-
-    tile = lax.fori_loop(0, DEPTH // 1536, slab, jnp.zeros((TOK, FEATS), F32))
-    token = lax.broadcasted_iota(jnp.int32, (TOK, FEATS), 0)
-    live = jnp.where(token < SLOT, cnt_ref[0], cnt_ref[1])
-    tile = jnp.where((token & (SLOT - 1)) < live, tile, 0.0)
-    rt[...] = tile.T.astype(BF16)
-    own_copy = pltpu.make_async_copy(rt, rb.at[slot], lsem.at[4])
-
-    swap_copy = copy(("swap",), rt, rb.at[c * NZ + z], swap)
-
-    send(("swap", 2), rt, rb.at[c * NZ + z], swap_to)
-
-    @pl.when(lone)
-    def _():
-        own_copy.start()
-        own_copy.wait()
-
-    @pl.when(jnp.logical_not(lone))
-    def _():
-        swap_copy.start()
-
     def rot_begin():
         @pl.when(jnp.logical_not(lone))
         def _():
@@ -236,10 +237,10 @@
     for it in range(1, 7):
         for item in grads:
             item.step(it)
-        if it == 4:
+        if it == 3:
             rot_begin()
-        if it >= 5:
-            rot.step(it - 4)
+        if it >= 4:
+            rot.step(it - 3)
         if it == 3:
             got(("b", "r", 0), bb.at[xl, top])
             send(("b", "rr"), bb.at[xl, top], bb.at[xl, top], dev(x=xr))
@@ -252,6 +253,8 @@
     grads[1].end()
     got(("b", "rr"), bb.at[xo, pl.ds(0, HALF)])
     got(("b", "ll"), bb.at[xo, pl.ds(HALF, HALF)])
+
+    early = len(sent)
 
     blocks = (xo, xr, xl, x)
 
@@ -306,7 +309,6 @@
     multiply(0)
     multiply(1)
     scatter(0)
-    rot.step(3)
     multiply(2)
     scatter(1)
     multiply(3)
@@ -333,6 +335,8 @@
     products(2)
     o2s[1, 0] = acc[2, top].astype(BF16)
     send(("o2", "l", 0), o2s.at[1, 0], o2r.at[1, 0], dev(x=xl))
+    for cp in sent[:early]:
+        cp.wait_send()
     got(("o1", "r"), o1r.at[0])
     o2s[0, 0] = (acc[1, top] + o1r[0].astype(F32)).astype(BF16)
     send(("o2", "r", 0), o2s.at[0, 0], o2r.at[0, 0], dev(x=xr))
@@ -340,6 +344,9 @@
     o2s[1, 1] = (acc[2, low] + o1r[1].astype(F32)).astype(BF16)
     send(("o2", "l", 1), o2s.at[1, 1], o2r.at[1, 1], dev(x=xl))
     collect(3)
+    for cp in sent[early : len(sent) - 8]:
+        cp.wait_send()
+    late = len(sent) - 8
     products(3)
     for w, way in ((0, "r"), (1, "l")):
         for h in (1 - w, w):
@@ -349,7 +356,7 @@
         total = acc[3, rows] + o2r[0, h].astype(F32) + o2r[1, h].astype(F32)
         out_ref[rows, :] = total * FACTOR
 
-    for cp in sent:
+    for cp in sent[late:]:
         cp.wait_send()
 
     @pl.when(jnp.logical_not(lone))
@@ -365,10 +372,9 @@
     return pl.pallas_call(
         kernel,
         out_shape=jax.ShapeDtypeStruct((COLS, WIDE), F32),
-        in_specs=[hbm, hbm, hbm, hbm, pl.BlockSpec(memory_space=pltpu.SMEM)],
+        in_specs=[vmem, hbm, hbm, hbm, pl.BlockSpec(memory_space=pltpu.SMEM)],
         out_specs=vmem,
         scratch_shapes=[
-            pltpu.VMEM((UNITS, NX * QUARTER), BF16),
             pltpu.VMEM((NX, 2, 32, PAIR), BF16),
             pltpu.VMEM((NX, 2, 32, PAIR), BF16),
             pltpu.VMEM((NX, 32, PAIR), BF16),
@@ -395,7 +401,7 @@
             pltpu.SemaphoreType.DMA((5,)),
         ],
         compiler_params=pltpu.CompilerParams(
-            collective_id=0, has_side_effects=True, vmem_limit_bytes=56 * 1024 * 1024
+            collective_id=0, has_side_effects=True, vmem_limit_bytes=53 * 1024 * 1024
         ),
         cost_estimate=pl.CostEstimate(
             flops=2_200_000_000, bytes_accessed=10_000_000, transcendentals=0

time: 82.6 us -> 81.6 us (0.988)
  Pallas kernels: 80.4 us -> 79.1 us
    pallas_call x1, Pallas kernels: 80.4 us -> 79.1 us  [shards(): pl.pallas_call(kernel, out_shape=jax.ShapeDtypeStruct((COLS, WIDE), F32),...]
    unnamed x1 -> x5, local copies, waits for them, and re-layouts: 1.84 us -> 2.33 us
where the time goes in v5:
time: 81.6 us; the launch traced here: 81.5 us
  Pallas kernels  79.1 us (97%)
  local copies, waits for them, and re-layouts  2.33 us (3%)
    pallas_call x1, Pallas kernels, shards(): pl.pallas_call(kernel, out_shape=jax.ShapeDtypeStruct((COLS, WIDE), F32),...  79.1 us
    unnamed x5, local copies, waits for them, and re-layouts  2.33 us

profile of v5, /device:TPU:1, one launch (start us, length us, event | category | flops | bytes accessed | tf_op | source)
XLA Modules:
  0.0 81.5 jit_solution(1089395529913941344)
XLA Ops:
  0.0 0.0 copy-start
  0.0 0.9 %copy-done = bf16[20,2048]{1,0:T(8,128)(2,1)S(1)} copy-done((bf16[20,2048]{1,0:T(8,128)(2,1)S(1)}, bf16[20,2048]{1,0:T(8,128)(2,1)}, u32[]{:S(2)}) %copy-start) | copy-done | bytes 81944
  0.9 0.0 copy-start.1
  0.9 0.7 copy-done.1
  1.5 79.1 %shard_map.55 = f32[160,768]{1,0:T(8,128)S(1)} custom-call(bf16[20,2048]{1,0:T(8,128)(2,1)S(1)} %copy-done, bf16[160,1920]{1,0:T(8,128)(2,1)} %bitcast.3, bf16[256,6144]{1,0:T(8,128)(2,1)} %in_ref.1, bf16[64,6144]{1,0:T(8,128)(2,1)} %bitcast.2, s32[2]{0:T(128)S(1)} %copy-done.1), custom_call_target="tpu_custom_call" | custom-call | flops 2200000000 | bytes 10000000 | tf_op jit(solution)/shard_map/pallas_call | solution.py:372
  80.7 0.8 copy.7
Async XLA Ops:
  0.0 0.9 %copy-start = (bf16[20,2048]{1,0:T(8,128)(2,1)S(1)}, bf16[20,2048]{1,0:T(8,128)(2,1)}, u32[]{:S(2)}) copy-start(bf16[20,2048]{1,0:T(8,128)(2,1)} %g_ref.1) | copy-start | bytes 245764
  0.9 0.7 copy-start.1

commit v6 on v5

--- a/solution.py
+++ b/solution.py
@@ -99,8 +99,9 @@
 
     pl.semaphore_wait(barrier, jnp.where(lone, len(peers), len(peers) + 1))
 
-    for n, xt in enumerate((xr, xl, xo)):
+    for n, xt in ((2, xo), (0, xr), (1, xl)):
         send(("a", n, 0), gs.at[xt], ga.at[x], dev(x=xt))
+    for n, xt in ((2, xo), (0, xr), (1, xl)):
         send(("a", n, 1), gs.at[xt, 1], go.at[x], dev(x=xt, yl=1 - yl))
     send(("a", 3, 1), gs.at[x, 1], go.at[x], pair_y)
     ga[x] = gs[x]
@@ -313,21 +314,21 @@
     scatter(1)
     multiply(3)
     scatter(2)
+    scatter(3)
+    rot.step(4)
     spread(0)
-    rot.step(4)
-    scatter(3)
     spread(1)
     rot.step(5)
+    spread(2)
     collect(0)
-    spread(2)
     rot.step(6)
+    spread(3)
     products(0)
     o1s[0] = acc[0, top].astype(BF16)
     send(("o1", "r"), o1s.at[0], o1r.at[0], dev(x=xr))
     o1s[1] = acc[0, low].astype(BF16)
     send(("o1", "l"), o1s.at[1], o1r.at[1], dev(x=xl))
     collect(1)
-    spread(3)
     products(1)
     o2s[0, 1] = acc[1, low].astype(BF16)
     send(("o2", "r", 1), o2s.at[0, 1], o2r.at[0, 1], dev(x=xr))

time: 81.6 us -> 81.5 us (level)
  no operation moved by 1% of the time
where the time goes in v6:
time: 81.5 us; the launch traced here: 80.9 us
  Pallas kernels  78.5 us (96%)
  local copies, waits for them, and re-layouts  2.33 us (3%)
    pallas_call x1, Pallas kernels, shards(): pl.pallas_call(kernel, out_shape=jax.ShapeDtypeStruct((COLS, WIDE), F32),...  78.5 us
    unnamed x5, local copies, waits for them, and re-layouts  2.33 us

profile of v6, /device:TPU:1, one launch (start us, length us, event | category | flops | bytes accessed | tf_op | source)
XLA Modules:
  0.0 80.9 jit_solution(12170803993862742780)
XLA Ops:
  0.0 0.0 copy-start
  0.0 0.9 %copy-done = bf16[20,2048]{1,0:T(8,128)(2,1)S(1)} copy-done((bf16[20,2048]{1,0:T(8,128)(2,1)S(1)}, bf16[20,2048]{1,0:T(8,128)(2,1)}, u32[]{:S(2)}) %copy-start) | copy-done | bytes 81944
  0.9 0.0 copy-start.1
  0.9 0.7 copy-done.1
  1.5 78.5 %shard_map.55 = f32[160,768]{1,0:T(8,128)S(1)} custom-call(bf16[20,2048]{1,0:T(8,128)(2,1)S(1)} %copy-done, bf16[160,1920]{1,0:T(8,128)(2,1)} %bitcast.3, bf16[256,6144]{1,0:T(8,128)(2,1)} %in_ref.1, bf16[64,6144]{1,0:T(8,128)(2,1)} %bitcast.2, s32[2]{0:T(128)S(1)} %copy-done.1), custom_call_target="tpu_custom_call" | custom-call | flops 2200000000 | bytes 10000000 | tf_op jit(solution)/shard_map/pallas_call | solution.py:373
  80.1 0.8 copy.7
Async XLA Ops:
  0.0 0.9 %copy-start = (bf16[20,2048]{1,0:T(8,128)(2,1)S(1)}, bf16[20,2048]{1,0:T(8,128)(2,1)}, u32[]{:S(2)}) copy-start(bf16[20,2048]{1,0:T(8,128)(2,1)} %g_ref.1) | copy-start | bytes 245764
  0.9 0.7 copy-start.1
